TPU v7x, 32 devices: a whole 2x2x4 slice. The times are simulated.
32 devices in a mesh: rep: 4 (over y, x), blk: 8 (over z, core).
Axes of the slice: x: 2, y: 2, z: 4, core: 2. Of those that a mesh axis runs over, the one named last changes fastest.
Arguments:
- node_features: bfloat16 [8192, 256], P(('rep', 'blk')), may hold values from -6 to 6
- tile_values: bfloat16 [4, 8, 16, 128, 128], P('rep', 'blk'), may hold values from -0.25 to 0.25
- tile_row: int32 [4, 8, 16], P('rep', 'blk'), may hold values from 0 to 7, as said below
- tile_col: int32 [4, 8, 16], P('rep', 'blk'), may hold values from 0 to 15
- tile_count: int32 [4, 8], P('rep', 'blk'), may hold values from 2 to 16, as said below
- weight: bfloat16 [256, 256], replicated, may hold values from -0.375 to 0.375
- cotangent: bfloat16 [8, 4, 256, 256], P('blk', 'rep'), may hold values from -6 to 6
Outputs:
- layer_out: bfloat16 [8, 4, 256, 256], P('blk', 'rep')
- grad_weight: float32 [256, 256], replicated
- grad_features: bfloat16 [8192, 256], P(('rep', 'blk'))
Inputs may be any that keep to these rules, and one draw needn't show every extreme that they name: `tile_row`: within one device the live slots name distinct tile pairs. Slots 0 to tile_count - 1 of a device are live, the rest are ignored; some device has all 16 slots live.
All inputs are finite; a program needn't handle non-finite values.
Results may differ from a plain program's by a relative error of at most 0.03.
Values may be sent and summed in bfloat16 or wider, within the bound.
A program may use at most 128 MiB of HBM per device.

v0:
```python
import jax
import jax.numpy as jnp
from jax import lax
from jax.sharding import PartitionSpec as P


def on_device(node_features, tile_values, tile_row, tile_col, tile_count, weight, cotangent):
    rows_dev, features = node_features.shape
    tile_block = tile_values[0, 0]
    slot_rows = tile_row[0, 0]
    slot_cols = tile_col[0, 0]
    live_count = tile_count[0, 0]
    slot_count = tile_block.shape[0]
    tile_size = tile_block.shape[1]
    rep_size = lax.axis_size("rep")
    slab_rows = rows_dev * rep_size
    slab_blocks = slab_rows // tile_size
    live_mask = (jnp.arange(slot_count, dtype=jnp.int32) < live_count).astype(jnp.float32)
    row_hot = (slot_rows[:, None] == jnp.arange(slab_blocks, dtype=jnp.int32)[None, :]).astype(
        jnp.float32
    ) * live_mask[:, None]
    gathered = lax.all_gather(node_features, "blk", axis=0, tiled=True)
    group_blocks = gathered.shape[0] // tile_size
    col_hot = (slot_cols[:, None] == jnp.arange(group_blocks, dtype=jnp.int32)[None, :]).astype(
        jnp.float32
    ) * live_mask[:, None]
    col_blocks = gathered.reshape(group_blocks, tile_size, features)
    picked = jnp.take(col_blocks, slot_cols, axis=0)
    products = jnp.einsum("tij,tjf->tif", tile_block, picked, preferred_element_type=jnp.float32)
    partial_value = (
        jnp.einsum("tk,tif->kif", row_hot, products)
        .reshape(slab_rows, features)
        .astype(jnp.bfloat16)
    )
    hidden_rows = (
        lax.psum_scatter(partial_value, "rep", scatter_dimension=0, tiled=True)
        .astype(jnp.float32)
        .astype(jnp.bfloat16)
    )
    preact = jnp.dot(hidden_rows, weight, preferred_element_type=jnp.float32)
    gating = jax.nn.sigmoid(preact)
    layer_out = (preact * gating).astype(jnp.bfloat16)
    slope_term = gating * (1.0 + preact * (1.0 - gating))
    grad_pre = (cotangent[0, 0].astype(jnp.float32) * slope_term).astype(jnp.bfloat16)
    weight_part = jnp.einsum("nf,ng->fg", hidden_rows, grad_pre, preferred_element_type=jnp.float32)
    grad_hidden = jnp.dot(grad_pre, weight.T, preferred_element_type=jnp.float32).astype(
        jnp.bfloat16
    )
    grad_slab = lax.all_gather(grad_hidden, "rep", axis=0, tiled=True)
    grad_weight = lax.psum(weight_part, ("rep", "blk"))
    grad_blocks = grad_slab.reshape(slab_blocks, tile_size, features)
    picked_rows = jnp.take(grad_blocks, slot_rows, axis=0)
    back_terms = jnp.einsum(
        "tij,tif->tjf", tile_block, picked_rows, preferred_element_type=jnp.float32
    )
    column_terms = (
        jnp.einsum("tk,tjf->kjf", col_hot, back_terms)
        .reshape(group_blocks * tile_size, features)
        .astype(jnp.bfloat16)
    )
    grad_features = (
        lax.psum_scatter(column_terms, "blk", scatter_dimension=0, tiled=True)
        .astype(jnp.float32)
        .astype(jnp.bfloat16)
    )
    return (layer_out.reshape(1, 1, rows_dev, features), grad_weight, grad_features)


def solution(mesh):
    placed = (
        P(("rep", "blk"), None),
        P("rep", "blk", None, None, None),
        P("rep", "blk", None),
        P("rep", "blk", None),
        P("rep", "blk"),
        P(),
        P("blk", "rep", None, None),
    )
    return jax.shard_map(
        on_device,
        mesh=mesh,
        in_specs=placed,
        out_specs=(P("blk", "rep", None, None), P(), P(("rep", "blk"), None)),
        check_vma=False,
    )
```

profile of v0, /device:TPU:0, one launch (start us, length us, event | category | flops | bytes accessed | tf_op | source)
XLA Modules:
  0.0 238.5 jit_solution(6410575573955138194)
XLA Ops:
  7.2 0.0 copy-start
  7.2 0.0 all-gather.2.cloned.1.call-start
  7.2 0.7 all-gather.2.cloned.1.call-update
  7.9 0.0 reduce-scatter.3.cloned.1.call-start
  8.6 0.6 copy-done.4
  9.3 25.2 %all-gather.2.cloned.1.call-done = bf16[2048,256]{1,0:T(8,128)(2,1)} async-done(((bf16[256,256]{1,0:T(8,128)(2,1)}), bf16[2048,256]{1,0:T(8,128)(2,1)}) %all-gather.2.cloned.1.call-update) | async-done | bytes 1048592 | tf_op jit(solution)/shard_map/all_gather | solution.py:22
  34.4 1.8 gather_fusion
  36.3 0.6 fusion.12
  36.9 0.9 copy.12
  37.8 0.0 copy-start.3
  37.8 0.6 copy-done.3
  38.4 0.3 fusion.7
  38.7 0.9 copy.10
  39.6 0.0 reduce-scatter.3.cloned.1.call-update
  39.6 0.0 all-reduce.2.cloned.1.call-start
  39.7 24.5 %reduce-scatter.3.cloned.1.call-done = bf16[256,256]{1,0:T(8,128)(2,1)} async-done(((bf16[1024,256]{1,0:T(8,128)(2,1)}), bf16[256,256]{1,0:T(8,128)(2,1)}) %reduce-scatter.3.cloned.1.call-update) | async-done | bytes 131088 | tf_op jit(solution)/shard_map/reduce_scatter | solution.py:36
  64.2 1.8 fusion.20
  66.1 0.2 convolution_convert_fusion
  66.3 0.7 copy-done.2
  67.0 0.9 fusion.38
  67.9 0.0 all-reduce.2.cloned.1.call-update
  67.9 0.0 reduce-scatter.5.cloned.1.call-start
  68.0 10.0 %all_gather.7 = bf16[1024,256]{1,0:T(8,128)(2,1)S(1)} all-gather(bf16[256,256]{1,0:T(8,128)(2,1)S(1)} %convolution_convert_fusion), channel_id=1, replica_groups=mesh['rep'=4,'blk'=8] {'rep'}, dimensions={0}, use_global_device_ids=true | all-gather | bytes 655360 | tf_op jit(solution)/shard_map/all_gather | solution.py:49
  77.9 0.6 gather_fusion.1
  78.6 0.6 fusion.10
  79.1 0.9 copy.13
  80.0 0.4 fusion.4
  80.4 1.3 copy.11
  81.8 0.0 reduce-scatter.5.cloned.1.call-update
  81.8 114.4 %all-reduce.2.cloned.1.call-done = f32[256,256]{1,0:T(8,128)} async-done(((f32[256,256]{1,0:T(8,128)}), f32[256,256]{1,0:T(8,128)}) %all-reduce.2.cloned.1.call-update) | async-done | bytes 262160 | tf_op jit(solution)/shard_map/psum | solution.py:50
  196.2 34.0 %reduce-scatter.5.cloned.1.call-done = bf16[256,256]{1,0:T(8,128)(2,1)} async-done(((bf16[2048,256]{1,0:T(8,128)(2,1)}), bf16[256,256]{1,0:T(8,128)(2,1)}) %reduce-scatter.5.cloned.1.call-update) | async-done | bytes 131088 | tf_op jit(solution)/shard_map/reduce_scatter | solution.py:62
  230.2 1.7 copy.16
  (14 shorter events, 0.1 us)
Async XLA Ops:
  7.2 29.1 %copy-start = (bf16[1,1,16,128,128]{4,3,2,1,0:T(8,128)(2,1)S(1)}, bf16[1,1,16,128,128]{4,3,2,1,0:T(8,128)(2,1)}, u32[]{:S(2)}) copy-start(bf16[1,1,16,128,128]{4,3,2,1,0:T(8,128)(2,1)} %param.8) | copy-start | bytes 1572868
  7.2 27.3 %all-gather.2.cloned.1.call-start = ((), (), s32[]{:S(2)}) async-start(), calls=%async_computation.2 | async-start | bytes 1179648 | tf_op jit(solution)/shard_map/all_gather | solution.py:22
  7.9 56.3 %reduce-scatter.3.cloned.1.call-start = ((), (), s32[]{:S(2)}) async-start(), calls=%async_computation.3 | async-start | bytes 655360 | tf_op jit(solution)/shard_map/reduce_scatter | solution.py:36
  8.6 0.7 copy-start.4
  37.8 0.7 copy-start.3
  39.6 24.6 %copy-start.1 = (bf16[256,256]{1,0:T(8,128)(2,1)S(1)}, bf16[256,256]{1,0:T(8,128)(2,1)}, u32[]{:S(2)}) copy-start(bf16[256,256]{1,0:T(8,128)(2,1)} %param.12) | copy-start | bytes 393220
  39.6 24.6 %copy-start.5 = (bf16[1,1,256,256]{3,2,1,0:T(8,128)(2,1)S(1)}, bf16[1,1,256,256]{3,2,1,0:T(8,128)(2,1)}, u32[]{:S(2)}) copy-start(bf16[1,1,256,256]{3,2,1,0:T(8,128)(2,1)} %param.13) | copy-start | bytes 393220
  39.6 156.6 %all-reduce.2.cloned.1.call-start = ((), (), s32[]{:S(2)}) async-start(), calls=%async_computation.4 | async-start | bytes 524288 | tf_op jit(solution)/shard_map/psum | solution.py:50
  66.1 0.9 copy-start.2
  67.9 162.3 %reduce-scatter.5.cloned.1.call-start = ((), (), s32[]{:S(2)}) async-start(), calls=%async_computation.5 | async-start | bytes 1179648 | tf_op jit(solution)/shard_map/reduce_scatter | solution.py:62
Sparse Core Ops, SparseCore 0:
  9.6 24.7 all-gather.1
  39.8 24.4 reduce-scatter.2
  71.2 124.9 all-reduce.1
  199.0 31.1 reduce-scatter.4
where the time goes:
time: 239 us; the launch traced here: 238 us
  waiting for transfers between devices  199 us (83%)
  between operations  14.5 us (6%)
  local copies, waits for them, and re-layouts  10.1 us (4%)
  blocking collectives  9.97 us (4%)
  matrix products  4.78 us (2%)
    psum x1, waiting for transfers between devices, on_device(): grad_weight = lax.psum(weight_part, ('rep', 'blk'))  114 us
    reduce_scatter x1, waiting for transfers between devices, on_device(): lax.psum_scatter(column_terms, 'blk', scatter_dimension=0, tiled=True)  34 us
    all_gather x1, waiting for transfers between devices, on_device(): gathered = lax.all_gather(node_features, 'blk', axis=0, tiled=True)  25.2 us
    reduce_scatter x1, waiting for transfers between devices, on_device(): lax.psum_scatter(partial_value, 'rep', scatter_dimension=0, tiled=True)  24.5 us
    all_gather x1, blocking collectives, on_device(): grad_slab = lax.all_gather(grad_hidden, 'rep', axis=0, tiled=True)  9.97 us
  transfers between devices with their start and end apart: 4, of which 4 were waited for; matrix products, arithmetic and copies ran while one was open for 2% of the time, Pallas kernels for 0%

commit v1 on v0

v1 whole, which is shorter than its diff:
```python
import functools

import jax
import jax.numpy as jnp
from jax import lax
from jax.experimental import pallas as pl
from jax.experimental.pallas import tpu as pltpu
from jax.sharding import PartitionSpec as P

MESH = pl.DeviceIdType.MESH
BF16, F32 = jnp.bfloat16, jnp.float32
PIECES = 1


def partner(index, step):
    out, bit = index, 1
    while bit <= step:
        if step & bit:
            out = out + bit * (1 - 2 * ((index // bit) % 2))
        bit *= 2
    return out


def kernel(
    n_rep, n_blk, pieces,
    slot_ref, tiles_hbm, x_hbm, w_hbm, cot_hbm,
    layer_ref, gw_ref, gf_ref,
    tiles, dense, xg, w, cot, acc, pout, pin, gg, bsib_out, bsib_in, bout, bin_, brelay,
    wsib_out, wsib_in, wl_out, wl_in, wr_in, wgath, wpart, fin,
    loc, xs, xr, ps, pr, gs, gr, bs, br_sib, br_line, br_relay, ws, wr,
):
    rows, feats = x_hbm.shape
    tile = tiles.shape[1]
    per = rows // tile
    line = n_blk // 2
    slab, group = rows * n_rep, rows * n_blk
    slab_blocks, group_blocks = slab // tile, group // tile
    fh = feats // pieces
    relay = line == 4
    r, b = lax.axis_index("rep"), lax.axis_index("blk")
    z, c = b // 2, b % 2
    other = b + 1 - 2 * c
    outer = jnp.logical_or(z == 0, z == line - 1)

    def blk_at(m):
        return partner(z, m) * 2 + c

    def remote(src, dst, send, recv, rep, blk):
        return pltpu.make_async_remote_copy(
            src_ref=src, dst_ref=dst, send_sem=send, recv_sem=recv,
            device_id={"rep": rep, "blk": blk}, device_id_type=MESH,
        )

    def arrive(dst, send, recv, rep, blk):
        remote(dst, dst, send, recv, rep, blk).wait_recv()

    fetch = [
        pltpu.make_async_copy(x_hbm, xg.at[b], loc.at[0]),
        pltpu.make_async_copy(tiles_hbm, tiles.at[pl.ds(1, tiles.shape[0] - 1)], loc.at[1]),
        pltpu.make_async_copy(w_hbm, w, loc.at[2]),
        pltpu.make_async_copy(cot_hbm, cot, loc.at[3]),
    ]
    for copy in fetch:
        copy.start()

    barrier = pltpu.get_barrier_semaphore()
    friends = [(r, blk_at(m)) for m in range(1, line)] + [(r, other)]
    friends += [(partner(r, m), b) for m in range(1, n_rep)]
    for rep, blk in friends:
        pl.semaphore_signal(
            barrier, inc=1, device_id={"rep": rep, "blk": blk}, device_id_type=MESH
        )
    tiles[0] = jnp.zeros((tile, tile), BF16)
    pl.semaphore_wait(barrier, len(friends))

    def cols(h):
        return pl.ds(h * fh, fh)

    sends = []

    def x_line(h, m):
        return remote(
            x_hbm.at[:, cols(h)], xg.at[b, :, cols(h)], xs.at[h, 0, m], xr.at[h, b], r, blk_at(m)
        )

    def x_relay(h):
        via = blk_at(2)
        return remote(
            xg.at[via, :, cols(h)], xg.at[via, :, cols(h)], xs.at[h, 0, 0], xr.at[h, via],
            r, blk_at(1),
        )

    def x_pass(h, m):
        blk = blk_at(m)
        src = x_hbm.at[:, cols(h)] if m == 0 else xg.at[blk, :, cols(h)]
        return remote(
            src, xg.at[blk, :, cols(h)], xs.at[h, 1, m], xr.at[h, blk], r, other
        )

    for h in range(pieces):
        for m in range(line - 1, 0, -1):
            if relay and m == 3:
                @pl.when(jnp.logical_not(outer))
                def _():
                    x_line(h, m).start()
            else:
                x_line(h, m).start()
        x_pass(h, 0).start()

    fetch[1].wait()

    def lay_out(n, carry):
        panel, k = n // slab_blocks, n % slab_blocks
        for j in range(per):
            slot = slot_ref[k * group_blocks + panel * per + j]
            start = pl.multiple_of(panel * slab + k * tile, tile)
            dense[pl.ds(start, tile), j * tile:(j + 1) * tile] = tiles[slot]
        return carry

    lax.fori_loop(0, n_blk * slab_blocks, lay_out, 0, unroll=4)
    fetch[0].wait()

    chunk = 4 * rows if slab % (4 * rows) == 0 else rows

    def add_panel(h, base, height, rhs, first):
        for at in range(0, height, chunk):
            lhs = dense[pl.ds(pl.multiple_of(base + at, tile), chunk), :]
            part = jnp.dot(lhs, rhs, preferred_element_type=F32)
            if first:
                acc[pl.ds(at, chunk), cols(h)] = part
            else:
                acc[pl.ds(at, chunk), cols(h)] += part

    def p_send(h, m):
        to = partner(r, m)
        return remote(
            pout.at[to, :, cols(h)], pin.at[r, :, cols(h)], ps.at[h, m], pr.at[h, r], to, b
        )

    for h in range(pieces):
        add_panel(h, b * slab, slab, xg[b, :, cols(h)], True)
        arrive(xg.at[other, :, cols(h)], xs.at[h, 1, 0], xr.at[h, other], r, other)
        add_panel(h, other * slab, slab, xg[other, :, cols(h)], False)
        for m in range(1, line):
            blk = blk_at(m)
            arrive(xg.at[blk, :, cols(h)], xs.at[h, 0, m], xr.at[h, blk], r, blk)
            if relay and m == 2:
                @pl.when(jnp.logical_not(outer))
                def _():
                    x_relay(h).start()
            x_pass(h, m).start()
            add_panel(h, blk * slab, slab, xg[blk, :, cols(h)], False)
            if m > 1:
                last = partner(z, m - 1) * 2 + 1 - c
                arrive(xg.at[last, :, cols(h)], xs.at[h, 1, m - 1], xr.at[h, last], r, other)
                add_panel(h, last * slab, slab, xg[last, :, cols(h)], False)
        last = partner(z, line - 1) * 2 + 1 - c
        arrive(xg.at[last, :, cols(h)], xs.at[h, 1, line - 1], xr.at[h, last], r, other)
        for m in range(n_rep - 1, -1, -1):
            to = partner(r, m)
            at = pl.multiple_of(to * rows, rows)
            panel = dense[pl.ds(pl.multiple_of(last * slab + to * rows, rows), rows), :]
            part = acc[pl.ds(at, rows), cols(h)] + jnp.dot(
                panel, xg[last, :, cols(h)], preferred_element_type=F32
            )
            pout[to, :, cols(h)] = part.astype(BF16)
            if m:
                p_send(h, m).start()

    def turn(t, carry):
        tiles[t] = tiles[t].T
        return carry

    lax.fori_loop(1, tiles.shape[0], turn, 0)

    def lay_out_turned(n, carry):
        panel, k = n // group_blocks, n % group_blocks
        for j in range(per):
            slot = slot_ref[(panel * per + j) * group_blocks + k]
            start = pl.multiple_of(panel * group + k * tile, tile)
            dense[pl.ds(start, tile), j * tile:(j + 1) * tile] = tiles[slot]
        return carry

    lax.fori_loop(0, n_rep * group_blocks, lay_out_turned, 0, unroll=4)
    fetch[2].wait()
    fetch[3].wait()

    total = pout[r].astype(F32)
    for m in range(1, n_rep):
        peer = partner(r, m)
        for h in range(pieces):
            arrive(pin.at[peer, :, cols(h)], ps.at[h, m], pr.at[h, peer], peer, b)
        total = total + pin[peer].astype(F32)
    hidden = total.astype(BF16)
    preact = jnp.dot(hidden, w[...], preferred_element_type=F32)
    gate = jax.nn.sigmoid(preact)
    slope = gate * (1.0 + preact * (1.0 - gate))
    grad_pre = (cot[...].astype(F32) * slope).astype(BF16)

    def g_send(h, m):
        to = partner(r, m)
        return remote(
            gg.at[r, :, cols(h)], gg.at[r, :, cols(h)], gs.at[h, m], gr.at[h, r], to, b
        )

    for h in range(pieces):
        gg[r, :, cols(h)] = lax.dot_general(
            grad_pre, w[cols(h), :], (((1,), (1,)), ((), ())), preferred_element_type=F32
        ).astype(BF16)
        for m in range(n_rep - 1, 0, -1):
            g_send(h, m).start()

    layer_ref[...] = (preact * gate).astype(BF16)
    wpart[...] = lax.dot_general(
        hidden, grad_pre, (((0,), (0,)), ((), ())), preferred_element_type=F32
    )
    half = feats // 2
    share = half // line
    kind = wl_out.dtype
    mine_at, other_at = c * half, (1 - c) * half
    wsib_out[...] = wpart[pl.ds(pl.multiple_of(other_at, half), half), :].astype(kind)
    w_sib = remote(wsib_out, wsib_in, ws.at[0, 0], wr.at[0, 0], r, other)
    w_sib.start()

    add_panel(0, r * group, group, gg[r, :, cols(0)], True)

    w_sib.wait_recv()
    both = wpart[pl.ds(pl.multiple_of(mine_at, half), half), :] + wsib_in[...].astype(F32)
    wpart[pl.ds(0, half), :] = both
    for m in range(line):
        at = pl.multiple_of(partner(z, m) * share, share)
        wl_out[m] = wpart[pl.ds(at, share), :].astype(kind)

    def w_line(m):
        return remote(wl_out.at[m], wl_in.at[m], ws.at[1, m], wr.at[1, m], r, blk_at(m))

    for m in range(1, line):
        w_line(m).start()

    def w_rep(m):
        return remote(
            wr_in.at[r], wr_in.at[r], ws.at[2, m], wr.at[2, r], partner(r, m), b
        )

    def w_sum_line():
        part = wl_out[0].astype(F32)
        for m in range(1, line):
            w_line(m).wait_recv()
            part = part + wl_in[m].astype(F32)
        wr_in[r] = part.astype(kind)
        for m in range(1, n_rep):
            w_rep(m).start()

    def w_back(m):
        return remote(
            wgath.at[c, z], wgath.at[c, z], ws.at[3, m], wr.at[3, z], r, blk_at(m)
        )

    def w_pass(m):
        place = partner(z, m)
        return remote(
            wgath.at[c, place], wgath.at[c, place], ws.at[4, m], wr.at[4, place], r, other
        )

    def w_sum_rep():
        for m in range(1, n_rep):
            peer = partner(r, m)
            arrive(wr_in.at[peer], ws.at[2, m], wr.at[2, peer], peer, b)
        part = wr_in[0].astype(F32)
        for i in range(1, n_rep):
            part = part + wr_in[i].astype(F32)
        wgath[c, z] = part.astype(kind)
        for m in range(1, line):
            w_back(m).start()
        w_pass(0).start()

    def b_sib(h, m):
        place = partner(z, m)
        return remote(
            bsib_out.at[place, :, cols(h)], bsib_in.at[place, :, cols(h)],
            bs.at[h, 0, m], br_sib.at[h, place], r, other,
        )

    def b_line(h, m):
        return remote(
            bout.at[m, :, cols(h)], bin_.at[m, :, cols(h)],
            bs.at[h, 1, m], br_line.at[h, m], r, blk_at(m),
        )

    def b_relay(h):
        return remote(
            bout.at[3, :, cols(h)], brelay.at[:, cols(h)],
            bs.at[h, 1, 3], br_relay.at[h], r, blk_at(2),
        )

    for h in range(pieces):
        if h:
            add_panel(h, r * group, group, gg[r, :, cols(h)], True)
        for m in range(1, n_rep):
            peer = partner(r, m)
            arrive(gg.at[peer, :, cols(h)], gs.at[h, m], gr.at[h, peer], peer, b)
            if m < n_rep - 1:
                add_panel(h, peer * group, group, gg[peer, :, cols(h)], False)
            if m == 1 and h == 0:
                w_sum_line()
        peer = partner(r, n_rep - 1)
        rhs = gg[peer, :, cols(h)]

        def finish(blk):
            at = pl.multiple_of(blk * rows, rows)
            panel = dense[pl.ds(pl.multiple_of(peer * group + blk * rows, rows), rows), :]
            return acc[pl.ds(at, rows), cols(h)] + jnp.dot(
                panel, rhs, preferred_element_type=F32
            )

        for m in range(line - 1, -1, -1):
            place = partner(z, m)
            bsib_out[place, :, cols(h)] = finish(place * 2 + 1 - c).astype(BF16)
            b_sib(h, m).start()
        if h == pieces - 1:
            w_sum_rep()
        for m in range(line - 1, -1, -1):
            place = partner(z, m)
            mine = finish(place * 2 + c)
            arrive(
                bsib_in.at[place, :, cols(h)], bs.at[h, 0, m], br_sib.at[h, place], r, other
            )
            mine = mine + bsib_in[place, :, cols(h)].astype(F32)
            if m == 0:
                fin[0, :, cols(h)] = mine
            elif relay and m == 3:
                bout[m, :, cols(h)] = mine.astype(BF16)

                @pl.when(outer)
                def _():
                    b_relay(h).start()

                @pl.when(jnp.logical_not(outer))
                def _():
                    b_line(h, m).start()
            elif relay and m == 1:
                fin[1, :, cols(h)] = mine

                @pl.when(jnp.logical_not(outer))
                def _():
                    b_relay(h).wait_recv()
                    fin[1, :, cols(h)] += brelay[:, cols(h)].astype(F32)

                bout[m, :, cols(h)] = fin[1, :, cols(h)].astype(BF16)
                b_line(h, m).start()
            else:
                bout[m, :, cols(h)] = mine.astype(BF16)
                b_line(h, m).start()

    for m in range(1, line):
        place = partner(z, m)
        arrive(wgath.at[c, place], ws.at[3, m], wr.at[3, place], r, blk_at(m))
        w_pass(m).start()

    for h in range(pieces):
        for m in range(1, line):
            if relay and m == 3:
                @pl.when(jnp.logical_not(outer))
                def _():
                    b_line(h, m).wait_recv()
                    fin[0, :, cols(h)] += bin_[m, :, cols(h)].astype(F32)
            else:
                b_line(h, m).wait_recv()
                fin[0, :, cols(h)] += bin_[m, :, cols(h)].astype(F32)
    gf_ref[...] = fin[0].astype(BF16)

    for m in range(line):
        place = partner(z, m)
        arrive(wgath.at[1 - c, place], ws.at[4, m], wr.at[4, place], r, other)
    for core in range(2):
        for place in range(line):
            at = core * half + place * share
            gw_ref[at:at + share, :] = wgath[core, place].astype(F32)

    for h in range(pieces):
        for m in range(1, line):
            if relay and m == 3:
                @pl.when(jnp.logical_not(outer))
                def _():
                    x_line(h, m).wait_send()
                    x_relay(h).wait_send()
            else:
                x_line(h, m).wait_send()
            b_line(h, m).wait_send()
        for m in range(line):
            x_pass(h, m).wait_send()
            b_sib(h, m).wait_send()
        for m in range(1, n_rep):
            p_send(h, m).wait_send()
            g_send(h, m).wait_send()
    w_sib.wait_send()
    for m in range(1, line):
        w_line(m).wait_send()
        w_back(m).wait_send()
    for m in range(line):
        w_pass(m).wait_send()
    for m in range(1, n_rep):
        w_rep(m).wait_send()


def on_device(n_rep, n_blk, node_features, tile_values, tile_row, tile_col, tile_count, weight, cotangent):
    rows, feats = node_features.shape
    slots, tile = tile_values.shape[2], tile_values.shape[3]
    slab_blocks = n_rep * rows // tile
    group_blocks = n_blk * rows // tile
    line = n_blk // 2
    share = feats // 2 // line
    kind = BF16 if share % 16 == 0 else F32
    number = jnp.arange(slots, dtype=jnp.int32)
    place = jnp.where(number < tile_count[0, 0], tile_row[0, 0] * group_blocks + tile_col[0, 0], -1)
    spots = jnp.arange(slab_blocks * group_blocks, dtype=jnp.int32)
    slot_of = jnp.max(
        jnp.where(place[:, None] == spots[None, :], number[:, None] + 1, 0), axis=0
    )
    block = (rows, feats)
    h = PIECES
    dma = pltpu.SemaphoreType.DMA
    layer, gw, gf = pl.pallas_call(
        functools.partial(kernel, n_rep, n_blk, h),
        out_shape=(
            jax.ShapeDtypeStruct(block, BF16),
            jax.ShapeDtypeStruct((feats, feats), F32),
            jax.ShapeDtypeStruct(block, BF16),
        ),
        in_specs=[pl.BlockSpec(memory_space=pltpu.SMEM)] + [pl.BlockSpec(memory_space=pl.ANY)] * 4,
        out_specs=tuple([pl.BlockSpec(memory_space=pltpu.VMEM)] * 3),
        scratch_shapes=[
            pltpu.VMEM((slots + 1, tile, tile), BF16),
            pltpu.VMEM((n_blk * n_rep * rows, rows), BF16),
            pltpu.VMEM((n_blk,) + block, BF16),
            pltpu.VMEM((feats, feats), BF16),
            pltpu.VMEM(block, BF16),
            pltpu.VMEM((max(n_blk, n_rep) * rows, feats), F32),
            pltpu.VMEM((n_rep,) + block, BF16),
            pltpu.VMEM((n_rep,) + block, BF16),
            pltpu.VMEM((n_rep,) + block, BF16),
            pltpu.VMEM((line,) + block, BF16),
            pltpu.VMEM((line,) + block, BF16),
            pltpu.VMEM((line,) + block, BF16),
            pltpu.VMEM((line,) + block, BF16),
            pltpu.VMEM(block, BF16),
            pltpu.VMEM((feats // 2, feats), kind),
            pltpu.VMEM((feats // 2, feats), kind),
            pltpu.VMEM((line, share, feats), kind),
            pltpu.VMEM((line, share, feats), kind),
            pltpu.VMEM((n_rep, share, feats), kind),
            pltpu.VMEM((2, line, share, feats), kind),
            pltpu.VMEM((feats, feats), F32),
            pltpu.VMEM((2,) + block, F32),
            dma((4,)),
            dma((h, 2, line)),
            dma((h, n_blk)),
            dma((h, n_rep)),
            dma((h, n_rep)),
            dma((h, n_rep)),
            dma((h, n_rep)),
            dma((h, 2, line)),
            dma((h, line)),
            dma((h, line)),
            dma((h,)),
            dma((5, max(line, n_rep))),
            dma((5, max(line, n_rep))),
        ],
        compiler_params=pltpu.CompilerParams(
            collective_id=0, has_side_effects=True, vmem_limit_bytes=62 * 1024 * 1024
        ),
    )(slot_of, tile_values[0, 0], node_features, weight, cotangent[0, 0])
    return layer.reshape((1, 1) + block), gw, gf


def solution(mesh):
    placed = (
        P(("rep", "blk"), None),
        P("rep", "blk", None, None, None),
        P("rep", "blk", None),
        P("rep", "blk", None),
        P("rep", "blk"),
        P(),
        P("blk", "rep", None, None),
    )
    return jax.shard_map(
        functools.partial(on_device, mesh.shape["rep"], mesh.shape["blk"]),
        mesh=mesh,
        in_specs=placed,
        out_specs=(P("blk", "rep", None, None), P(), P(("rep", "blk"), None)),
        check_vma=False,
    )
```

time: 239 us -> 59.3 us (0.25)
  waiting for transfers between devices: 199 us -> 0 us
  Pallas kernels: 0 us -> 53.3 us
  between operations: 14.5 us -> 1.31 us
  blocking collectives: 9.97 us -> 0 us
  local copies, waits for them, and re-layouts: 10.1 us -> 3.92 us
  matrix products: 4.78 us -> 0 us
    psum x1 -> x0, waiting for transfers between devices: 114 us -> none  [on_device(): grad_weight = lax.psum(weight_part, ('rep', 'blk'))]
    reduce_scatter x2 -> x0, waiting for transfers between devices: 58.5 us -> none  [the longest x1 34 us: on_device(): lax.psum_scatter(column_terms, 'blk', scatter_dimension=0, tiled=True)]
    pallas_call x0 -> x1, Pallas kernels: none -> 53.3 us  [on_device(): pl.pallas_call(functools.partial(kernel, n_rep, n_blk, h), out_shape=(jax...]
    all_gather x1 -> x0, waiting for transfers between devices: 25.2 us -> none  [on_device(): gathered = lax.all_gather(node_features, 'blk', axis=0, tiled=True)]
    all_gather x1 -> x0, blocking collectives: 9.97 us -> none  [on_device(): grad_slab = lax.all_gather(grad_hidden, 'rep', axis=0, tiled=True)]
    dot_general x7 -> x0, matrix products: 4.78 us -> none  [the longest x1 1.84 us: on_device(): preact = jnp.dot(hidden_rows, weight, preferred_element_type=jnp.float32)]
    gather x2 -> x0, local copies, waits for them, and re-layouts: 2.45 us -> none  [the longest x1 1.84 us: on_device(): picked = jnp.take(col_blocks, slot_cols, axis=0)]
  transfers between devices with their start and end apart: 4 -> 0, of which waited for: 4 -> 0; matrix products, arithmetic and copies ran while one was open for 2% -> 0% of each run, Pallas kernels for 0% -> 0%
where the time goes in v1:
time: 59.3 us; the launch traced here: 59.1 us
  Pallas kernels  53.3 us (90%)
  local copies, waits for them, and re-layouts  3.92 us (7%)
  between operations  1.31 us (2%)
  other arithmetic  0.6 us (1%)
    pallas_call x1, Pallas kernels, on_device(): pl.pallas_call(functools.partial(kernel, n_rep, n_blk, h), out_shape=(jax...  53.3 us
    unnamed x11, local copies, waits for them, and re-layouts  3.92 us

profile of v1, /device:TPU:0, one launch (start us, length us, event | category | flops | bytes accessed | tf_op | source)
XLA Modules:
  0.0 59.1 jit_solution(5985443920499095748)
XLA Ops:
  1.3 0.0 copy-start.2
  1.3 0.0 copy-start.3
  1.3 0.6 %copy-done.2 = s32[1,1,16]{2,1,0:T(1,128)S(1)} copy-done((s32[1,1,16]{2,1,0:T(1,128)S(1)}, s32[1,1,16]{2,1,0:T(1,128)}, u32[]{:S(2)}) %copy-start.2) | copy-done | bytes 88
  1.9 0.0 copy-done.3
  2.0 0.6 %select_reduce_fusion.slot_ref = s32[128]{0:T(128)} fusion(s32[16]{0:T(128)S(1)} %get-tuple-element.10, s32[16]{0:T(128)S(1)} %get-tuple-element.9), kind=kLoop, calls=%fused_computation | loop fusion | flops 6016 | bytes 640 | tf_op jit(solution)/shard_map/reduce_max | solution.py:417
  2.6 53.3 %shard_map.94 = (bf16[256,256]{1,0:T(8,128)(2,1)}, f32[256,256]{1,0:T(8,128)}, bf16[256,256]{1,0:T(8,128)(2,1)}) custom-call(s32[128]{0:T(128)} %select_reduce_fusion.slot_ref, bf16[16,128,128]{2,1,0:T(8,128)(2,1)} %bitcast.7, bf16[256,256]{1,0:T(8,128)(2,1)} %x_hbm.1, bf16[256,256]{1,0:T(8,128)(2,1)} %w_hbm.1, bf16[256,256]{1,0:T(8,128)(2,1)} %bitcast.8), custom_call_target="tpu_custom_call" | custom-call | tf_op jit(solution)/shard_map/pallas_call | solution.py:423
  55.8 0.0 copy-start
  55.8 1.6 %copy.14 = bf16[1,1,256,256]{3,2,1,0:T(8,128)(2,1)} copy(bf16[1,1,256,256]{3,2,1,0:T(8,128)(2,1)} %bitcast.9) | data formatting | bytes 262144
  57.5 0.0 copy-done
  57.5 0.0 copy-start.1
  57.5 0.7 %copy.15 = f32[256,256]{1,0:T(8,128)} copy(f32[256,256]{1,0:T(8,128)S(1)} %copy-done) | data formatting | bytes 524288
  58.2 0.3 copy-done.1
  58.5 0.7 %copy.16 = bf16[256,256]{1,0:T(8,128)(2,1)} copy(bf16[256,256]{1,0:T(8,128)(2,1)S(1)} %copy-done.1) | data formatting | bytes 262144
  (1 shorter events, 0.0 us)
Async XLA Ops:
  1.3 0.7 %copy-start.2 = (s32[1,1,16]{2,1,0:T(1,128)S(1)}, s32[1,1,16]{2,1,0:T(1,128)}, u32[]{:S(2)}) copy-start(s32[1,1,16]{2,1,0:T(1,128)} %param.10) | copy-start | bytes 196
  1.3 0.7 %copy-start.3 = (s32[1,1,16]{2,1,0:T(1,128)S(1)}, s32[1,1,16]{2,1,0:T(1,128)}, u32[]{:S(2)}) copy-start(s32[1,1,16]{2,1,0:T(1,128)} %param.9) | copy-start | bytes 196
  55.8 1.6 %copy-start = (f32[256,256]{1,0:T(8,128)S(1)}, f32[256,256]{1,0:T(8,128)}, u32[]{:S(2)}) copy-start(f32[256,256]{1,0:T(8,128)} %get-tuple-element.15) | copy-start | bytes 786436
  57.5 1.0 %copy-start.1 = (bf16[256,256]{1,0:T(8,128)(2,1)S(1)}, bf16[256,256]{1,0:T(8,128)(2,1)}, u32[]{:S(2)}) copy-start(bf16[256,256]{1,0:T(8,128)(2,1)} %get-tuple-element.16) | copy-start | bytes 393220

commit v2 on v1

--- a/solution.py
+++ b/solution.py
@@ -9,7 +9,7 @@
 
 MESH = pl.DeviceIdType.MESH
 BF16, F32 = jnp.bfloat16, jnp.float32
-PIECES = 1
+PIECES = 2
 
 
 def partner(index, step):

time: 59.3 us -> 56.5 us (0.953)
  Pallas kernels: 53.3 us -> 50.5 us
    pallas_call x1, Pallas kernels: 53.3 us -> 50.5 us  [on_device(): pl.pallas_call(functools.partial(kernel, n_rep, n_blk, h), out_shape=(jax...]
where the time goes in v2:
time: 56.5 us; the launch traced here: 56.3 us
  Pallas kernels  50.5 us (89%)
  local copies, waits for them, and re-layouts  3.92 us (7%)
  between operations  1.31 us (2%)
  other arithmetic  0.6 us (1%)
    pallas_call x1, Pallas kernels, on_device(): pl.pallas_call(functools.partial(kernel, n_rep, n_blk, h), out_shape=(jax...  50.5 us
    unnamed x11, local copies, waits for them, and re-layouts  3.92 us

profile of v2, /device:TPU:0, one launch (start us, length us, event | category | flops | bytes accessed | tf_op | source)
XLA Modules:
  0.0 56.3 jit_solution(16795090938422617268)
XLA Ops:
  1.3 0.0 copy-start.2
  1.3 0.0 copy-start.3
  1.3 0.6 %copy-done.2 = s32[1,1,16]{2,1,0:T(1,128)S(1)} copy-done((s32[1,1,16]{2,1,0:T(1,128)S(1)}, s32[1,1,16]{2,1,0:T(1,128)}, u32[]{:S(2)}) %copy-start.2) | copy-done | bytes 88
  1.9 0.0 copy-done.3
  2.0 0.6 %select_reduce_fusion.slot_ref = s32[128]{0:T(128)} fusion(s32[16]{0:T(128)S(1)} %get-tuple-element.10, s32[16]{0:T(128)S(1)} %get-tuple-element.9), kind=kLoop, calls=%fused_computation | loop fusion | flops 6016 | bytes 640 | tf_op jit(solution)/shard_map/reduce_max | solution.py:417
  2.6 50.5 %shard_map.94 = (bf16[256,256]{1,0:T(8,128)(2,1)}, f32[256,256]{1,0:T(8,128)}, bf16[256,256]{1,0:T(8,128)(2,1)}) custom-call(s32[128]{0:T(128)} %select_reduce_fusion.slot_ref, bf16[16,128,128]{2,1,0:T(8,128)(2,1)} %bitcast.7, bf16[256,256]{1,0:T(8,128)(2,1)} %x_hbm.1, bf16[256,256]{1,0:T(8,128)(2,1)} %w_hbm.1, bf16[256,256]{1,0:T(8,128)(2,1)} %bitcast.8), custom_call_target="tpu_custom_call" | custom-call | tf_op jit(solution)/shard_map/pallas_call | solution.py:423
  53.1 0.0 copy-start
  53.1 1.6 %copy.14 = bf16[1,1,256,256]{3,2,1,0:T(8,128)(2,1)} copy(bf16[1,1,256,256]{3,2,1,0:T(8,128)(2,1)} %bitcast.9) | data formatting | bytes 262144
  54.7 0.0 copy-done
  54.7 0.0 copy-start.1
  54.7 0.7 %copy.15 = f32[256,256]{1,0:T(8,128)} copy(f32[256,256]{1,0:T(8,128)S(1)} %copy-done) | data formatting | bytes 524288
  55.4 0.3 copy-done.1
  55.7 0.7 %copy.16 = bf16[256,256]{1,0:T(8,128)(2,1)} copy(bf16[256,256]{1,0:T(8,128)(2,1)S(1)} %copy-done.1) | data formatting | bytes 262144
  (1 shorter events, 0.0 us)
Async XLA Ops:
  1.3 0.7 %copy-start.2 = (s32[1,1,16]{2,1,0:T(1,128)S(1)}, s32[1,1,16]{2,1,0:T(1,128)}, u32[]{:S(2)}) copy-start(s32[1,1,16]{2,1,0:T(1,128)} %param.10) | copy-start | bytes 196
  1.3 0.7 %copy-start.3 = (s32[1,1,16]{2,1,0:T(1,128)S(1)}, s32[1,1,16]{2,1,0:T(1,128)}, u32[]{:S(2)}) copy-start(s32[1,1,16]{2,1,0:T(1,128)} %param.9) | copy-start | bytes 196
  53.1 1.6 %copy-start = (f32[256,256]{1,0:T(8,128)S(1)}, f32[256,256]{1,0:T(8,128)}, u32[]{:S(2)}) copy-start(f32[256,256]{1,0:T(8,128)} %get-tuple-element.15) | copy-start | bytes 786436
  54.7 1.0 %copy-start.1 = (bf16[256,256]{1,0:T(8,128)(2,1)S(1)}, bf16[256,256]{1,0:T(8,128)(2,1)}, u32[]{:S(2)}) copy-start(bf16[256,256]{1,0:T(8,128)(2,1)} %get-tuple-element.16) | copy-start | bytes 393220

commit v3 on v2

--- a/solution.py
+++ b/solution.py
@@ -23,8 +23,9 @@
 
 def kernel(
     n_rep, n_blk, pieces,
-    slot_ref, tiles_hbm, x_hbm, w_hbm, cot_hbm,
-    layer_ref, gw_ref, gf_ref,
+    row_ref, col_ref, count_ref, tiles_hbm, x_hbm, w_hbm, cot_hbm,
+    layer_hbm, gw_hbm, gf_hbm,
+    slot_vec, slot_ref, layer_ref, gw_ref, gf_ref,
     tiles, dense, xg, w, cot, acc, pout, pin, gg, bsib_out, bsib_in, bout, bin_, brelay,
     wsib_out, wsib_in, wl_out, wl_in, wr_in, wgath, wpart, fin,
     loc, xs, xr, ps, pr, gs, gr, bs, br_sib, br_line, br_relay, ws, wr,
@@ -71,6 +72,21 @@
             barrier, inc=1, device_id={"rep": rep, "blk": blk}, device_id_type=MESH
         )
     tiles[0] = jnp.zeros((tile, tile), BF16)
+
+    shape = slot_vec.shape
+    spots = lax.broadcasted_iota(jnp.int32, shape, 0) * shape[1] + lax.broadcasted_iota(
+        jnp.int32, shape, 1
+    )
+
+    def mark(t, found):
+        named = jnp.where(t < count_ref[0, 0], row_ref[t] * group_blocks + col_ref[t], -1)
+        return jnp.where(spots == named, t + 1, found)
+
+    slot_vec[...] = lax.fori_loop(
+        0, row_ref.shape[0], mark, jnp.zeros(shape, jnp.int32), unroll=8
+    )
+    slots_in = pltpu.make_async_copy(slot_vec, slot_ref, loc.at[4])
+    slots_in.start()
     pl.semaphore_wait(barrier, len(friends))
 
     def cols(h):
@@ -108,11 +124,15 @@
         x_pass(h, 0).start()
 
     fetch[1].wait()
+    slots_in.wait()
+
+    def slot_at(pair):
+        return slot_ref[pair // shape[1], pair % shape[1]]
 
     def lay_out(n, carry):
         panel, k = n // slab_blocks, n % slab_blocks
         for j in range(per):
-            slot = slot_ref[k * group_blocks + panel * per + j]
+            slot = slot_at(k * group_blocks + panel * per + j)
             start = pl.multiple_of(panel * slab + k * tile, tile)
             dense[pl.ds(start, tile), j * tile:(j + 1) * tile] = tiles[slot]
         return carry
@@ -176,7 +196,7 @@
     def lay_out_turned(n, carry):
         panel, k = n // group_blocks, n % group_blocks
         for j in range(per):
-            slot = slot_ref[(panel * per + j) * group_blocks + k]
+            slot = slot_at((panel * per + j) * group_blocks + k)
             start = pl.multiple_of(panel * group + k * tile, tile)
             dense[pl.ds(start, tile), j * tile:(j + 1) * tile] = tiles[slot]
         return carry
@@ -211,6 +231,8 @@
             g_send(h, m).start()
 
     layer_ref[...] = (preact * gate).astype(BF16)
+    layer_out = pltpu.make_async_copy(layer_ref, layer_hbm, loc.at[5])
+    layer_out.start()
     wpart[...] = lax.dot_general(
         hidden, grad_pre, (((0,), (0,)), ((), ())), preferred_element_type=F32
     )
@@ -356,19 +378,6 @@
         place = partner(z, m)
         arrive(wgath.at[c, place], ws.at[3, m], wr.at[3, place], r, blk_at(m))
         w_pass(m).start()
-
-    for h in range(pieces):
-        for m in range(1, line):
-            if relay and m == 3:
-                @pl.when(jnp.logical_not(outer))
-                def _():
-                    b_line(h, m).wait_recv()
-                    fin[0, :, cols(h)] += bin_[m, :, cols(h)].astype(F32)
-            else:
-                b_line(h, m).wait_recv()
-                fin[0, :, cols(h)] += bin_[m, :, cols(h)].astype(F32)
-    gf_ref[...] = fin[0].astype(BF16)
-
     for m in range(line):
         place = partner(z, m)
         arrive(wgath.at[1 - c, place], ws.at[4, m], wr.at[4, place], r, other)
@@ -376,6 +385,22 @@
         for place in range(line):
             at = core * half + place * share
             gw_ref[at:at + share, :] = wgath[core, place].astype(F32)
+    gw_out = pltpu.make_async_copy(gw_ref, gw_hbm, loc.at[6])
+    gw_out.start()
+
+    for h in range(pieces):
+        for m in range(1, line):
+            if relay and m == 3:
+                @pl.when(jnp.logical_not(outer))
+                def _():
+                    b_line(h, m).wait_recv()
+                    fin[0, :, cols(h)] += bin_[m, :, cols(h)].astype(F32)
+            else:
+                b_line(h, m).wait_recv()
+                fin[0, :, cols(h)] += bin_[m, :, cols(h)].astype(F32)
+    gf_ref[...] = fin[0].astype(BF16)
+    gf_out = pltpu.make_async_copy(gf_ref, gf_hbm, loc.at[7])
+    gf_out.start()
 
     for h in range(pieces):
         for m in range(1, line):
@@ -403,6 +428,21 @@
         w_rep(m).wait_send()
 
 
+    for copy in (layer_out, gw_out, gf_out):
+        copy.wait()
+
+
+def hand_over(layer, gw, gf, layer_to, gw_to, gf_to, sems):
+    copies = [
+        pltpu.make_async_copy(src, dst, sems.at[i])
+        for i, (src, dst) in enumerate([(layer, layer_to), (gw, gw_to), (gf, gf_to)])
+    ]
+    for copy in copies:
+        copy.start()
+    for copy in copies:
+        copy.wait()
+
+
 def on_device(n_rep, n_blk, node_features, tile_values, tile_row, tile_col, tile_count, weight, cotangent):
     rows, feats = node_features.shape
     slots, tile = tile_values.shape[2], tile_values.shape[3]
@@ -411,25 +451,29 @@
     line = n_blk // 2
     share = feats // 2 // line
     kind = BF16 if share % 16 == 0 else F32
-    number = jnp.arange(slots, dtype=jnp.int32)
-    place = jnp.where(number < tile_count[0, 0], tile_row[0, 0] * group_blocks + tile_col[0, 0], -1)
-    spots = jnp.arange(slab_blocks * group_blocks, dtype=jnp.int32)
-    slot_of = jnp.max(
-        jnp.where(place[:, None] == spots[None, :], number[:, None] + 1, 0), axis=0
-    )
+    pairs = slab_blocks * group_blocks
+    table = (-(-pairs // 1024) * 8, 128)
     block = (rows, feats)
     h = PIECES
     dma = pltpu.SemaphoreType.DMA
-    layer, gw, gf = pl.pallas_call(
+    results = (
+        jax.ShapeDtypeStruct(block, BF16),
+        jax.ShapeDtypeStruct((feats, feats), F32),
+        jax.ShapeDtypeStruct(block, BF16),
+    )
+    anywhere = pl.BlockSpec(memory_space=pl.ANY)
+    scalars = pl.BlockSpec(memory_space=pltpu.SMEM)
+    made = pl.pallas_call(
         functools.partial(kernel, n_rep, n_blk, h),
-        out_shape=(
-            jax.ShapeDtypeStruct(block, BF16),
-            jax.ShapeDtypeStruct((feats, feats), F32),
-            jax.ShapeDtypeStruct(block, BF16),
-        ),
-        in_specs=[pl.BlockSpec(memory_space=pltpu.SMEM)] + [pl.BlockSpec(memory_space=pl.ANY)] * 4,
-        out_specs=tuple([pl.BlockSpec(memory_space=pltpu.VMEM)] * 3),
+        out_shape=results,
+        in_specs=[scalars] * 3 + [anywhere] * 4,
+        out_specs=(anywhere,) * 3,
         scratch_shapes=[
+            pltpu.VMEM(table, jnp.int32),
+            pltpu.SMEM(table, jnp.int32),
+            pltpu.VMEM(block, BF16),
+            pltpu.VMEM((feats, feats), F32),
+            pltpu.VMEM(block, BF16),
             pltpu.VMEM((slots + 1, tile, tile), BF16),
             pltpu.VMEM((n_blk * n_rep * rows, rows), BF16),
             pltpu.VMEM((n_blk,) + block, BF16),
@@ -452,7 +496,7 @@
             pltpu.VMEM((2, line, share, feats), kind),
             pltpu.VMEM((feats, feats), F32),
             pltpu.VMEM((2,) + block, F32),
-            dma((4,)),
+            dma((8,)),
             dma((h, 2, line)),
             dma((h, n_blk)),
             dma((h, n_rep)),
@@ -469,7 +513,18 @@
         compiler_params=pltpu.CompilerParams(
             collective_id=0, has_side_effects=True, vmem_limit_bytes=62 * 1024 * 1024
         ),
-    )(slot_of, tile_values[0, 0], node_features, weight, cotangent[0, 0])
+    )(
+        tile_row[0, 0], tile_col[0, 0], tile_count, tile_values[0, 0],
+        node_features, weight, cotangent[0, 0],
+    )
+    layer, gw, gf = pl.pallas_call(
+        hand_over,
+        out_shape=results,
+        in_specs=[anywhere] * 3,
+        out_specs=(anywhere,) * 3,
+        scratch_shapes=[dma((3,))],
+        compiler_params=pltpu.CompilerParams(vmem_limit_bytes=62 * 1024 * 1024),
+    )(*made)
     return layer.reshape((1, 1) + block), gw, gf
 
 

time: 56.5 us -> 68.8 us (1.22)
  Pallas kernels: 50.5 us -> 67.3 us
  local copies, waits for them, and re-layouts: 3.92 us -> 0 us
    pallas_call x1 -> x2, Pallas kernels: 50.5 us -> 67.3 us  [the longest x1 50.3 us: on_device(): pl.pallas_call(functools.partial(kernel, n_rep, n_blk, h), out_shape=resu...]
    unnamed x11 -> x0, local copies, waits for them, and re-layouts: 3.92 us -> none
where the time goes in v3:
time: 68.8 us; the launch traced here: 68.6 us
  Pallas kernels  67.3 us (98%)
  between operations  1.29 us (2%)
    pallas_call x1, Pallas kernels, on_device(): pl.pallas_call(functools.partial(kernel, n_rep, n_blk, h), out_shape=resu...  50.3 us
    pallas_call x1, Pallas kernels, on_device(): pl.pallas_call(hand_over, out_shape=results, in_specs=[anywhere] * 3, out...  17 us

profile of v3, /device:TPU:0, one launch (start us, length us, event | category | flops | bytes accessed | tf_op | source)
XLA Modules:
  0.0 68.6 jit_solution(731544464530922281)
XLA Ops:
  1.3 50.3 %shard_map.94 = (bf16[256,256]{1,0:T(8,128)(2,1)}, f32[256,256]{1,0:T(8,128)}, bf16[256,256]{1,0:T(8,128)(2,1)}) custom-call(s32[16]{0:T(128)} %bitcast.7, s32[16]{0:T(128)} %bitcast.8, s32[1,1]{1,0:T(1,128)S(6)} %copy.10.count_ref, bf16[16,128,128]{2,1,0:T(8,128)(2,1)} %bitcast.5, bf16[256,256]{1,0:T(8,128)(2,1)} %x_hbm.1, bf16[256,256]{1,0:T(8,128)(2,1)} %w_hbm.1, ...), custom_call_target="tpu_custom_call" | custom-call | tf_op jit(solution)/shard_map/pallas_call | solution.py:466
  51.6 17.0 %shard_map.95 = (bf16[256,256]{1,0:T(8,128)(2,1)}, f32[256,256]{1,0:T(8,128)}, bf16[256,256]{1,0:T(8,128)(2,1)}) custom-call(bf16[256,256]{1,0:T(8,128)(2,1)} %get-tuple-element.9.layer, f32[256,256]{1,0:T(8,128)} %get-tuple-element.10.gw, bf16[256,256]{1,0:T(8,128)(2,1)} %get-tuple-element.11.gf), custom_call_target="tpu_custom_call" | custom-call | tf_op jit(solution)/shard_map/pallas_call | solution.py:520

commit v4 on v3

--- a/solution.py
+++ b/solution.py
@@ -26,12 +26,13 @@
     row_ref, col_ref, count_ref, tiles_hbm, x_hbm, w_hbm, cot_hbm,
     layer_hbm, gw_hbm, gf_hbm,
     slot_vec, slot_ref, layer_ref, gw_ref, gf_ref,
-    tiles, dense, xg, w, cot, acc, pout, pin, gg, bsib_out, bsib_in, bout, bin_, brelay,
+    tiles, slabs, xg, w, cot, acc, pout, pin, gg, bsib_out, bsib_in, bout, bin_, brelay,
     wsib_out, wsib_in, wl_out, wl_in, wr_in, wgath, wpart, fin,
     loc, xs, xr, ps, pr, gs, gr, bs, br_sib, br_line, br_relay, ws, wr,
 ):
     rows, feats = x_hbm.shape
     tile = tiles.shape[1]
+    dense, turned = slabs.at[0], slabs.at[slabs.shape[0] - 1]
     per = rows // tile
     line = n_blk // 2
     slab, group = rows * n_rep, rows * n_blk
@@ -56,12 +57,15 @@
         remote(dst, dst, send, recv, rep, blk).wait_recv()
 
     fetch = [
-        pltpu.make_async_copy(x_hbm, xg.at[b], loc.at[0]),
         pltpu.make_async_copy(tiles_hbm, tiles.at[pl.ds(1, tiles.shape[0] - 1)], loc.at[1]),
         pltpu.make_async_copy(w_hbm, w, loc.at[2]),
         pltpu.make_async_copy(cot_hbm, cot, loc.at[3]),
     ]
-    for copy in fetch:
+    x_in = [
+        pltpu.make_async_copy(x_hbm.at[:, pl.ds(h * fh, fh)], xg.at[b, h], loc.at[8 + h])
+        for h in range(pieces)
+    ]
+    for copy in x_in + fetch:
         copy.start()
 
     barrier = pltpu.get_barrier_semaphore()
@@ -96,24 +100,25 @@
 
     def x_line(h, m):
         return remote(
-            x_hbm.at[:, cols(h)], xg.at[b, :, cols(h)], xs.at[h, 0, m], xr.at[h, b], r, blk_at(m)
+            xg.at[b, h], xg.at[b, h], xs.at[h, 0, m], xr.at[h, b], r, blk_at(m)
         )
 
     def x_relay(h):
         via = blk_at(2)
         return remote(
-            xg.at[via, :, cols(h)], xg.at[via, :, cols(h)], xs.at[h, 0, 0], xr.at[h, via],
+            xg.at[via, h], xg.at[via, h], xs.at[h, 0, 0], xr.at[h, via],
             r, blk_at(1),
         )
 
     def x_pass(h, m):
         blk = blk_at(m)
-        src = x_hbm.at[:, cols(h)] if m == 0 else xg.at[blk, :, cols(h)]
-        return remote(
-            src, xg.at[blk, :, cols(h)], xs.at[h, 1, m], xr.at[h, blk], r, other
-        )
-
-    for h in range(pieces):
+        src = xg.at[blk, h]
+        return remote(
+            src, xg.at[blk, h], xs.at[h, 1, m], xr.at[h, blk], r, other
+        )
+
+    for h in range(pieces):
+        x_in[h].wait()
         for m in range(line - 1, 0, -1):
             if relay and m == 3:
                 @pl.when(jnp.logical_not(outer))
@@ -123,7 +128,7 @@
                 x_line(h, m).start()
         x_pass(h, 0).start()
 
-    fetch[1].wait()
+    fetch[0].wait()
     slots_in.wait()
 
     def slot_at(pair):
@@ -138,13 +143,37 @@
         return carry
 
     lax.fori_loop(0, n_blk * slab_blocks, lay_out, 0, unroll=4)
-    fetch[0].wait()
+
+    def turn(t, carry):
+        tiles[t] = tiles[t].T
+        return carry
+
+    def lay_out_turned(n, carry):
+        panel, k = n // group_blocks, n % group_blocks
+        for j in range(per):
+            slot = slot_at((panel * per + j) * group_blocks + k)
+            start = pl.multiple_of(panel * group + k * tile, tile)
+            turned[pl.ds(start, tile), j * tile:(j + 1) * tile] = tiles[slot]
+        return carry
+
+    def steps(body, first, last, count, unroll):
+        size = (last - first) // count
+        return [
+            functools.partial(
+                lax.fori_loop, first + i * size, first + (i + 1) * size, body, 0, unroll=unroll
+            )
+            for i in range(count)
+        ]
+
+    later = steps(turn, 1, tiles.shape[0], 2, 2)
+    later += steps(lay_out_turned, 0, n_rep * group_blocks, 4, 4)
+    early = slabs.shape[0] > 1
 
     chunk = 4 * rows if slab % (4 * rows) == 0 else rows
 
-    def add_panel(h, base, height, rhs, first):
+    def add_panel(slabs, h, base, height, rhs, first):
         for at in range(0, height, chunk):
-            lhs = dense[pl.ds(pl.multiple_of(base + at, tile), chunk), :]
+            lhs = slabs[pl.ds(pl.multiple_of(base + at, tile), chunk), :]
             part = jnp.dot(lhs, rhs, preferred_element_type=F32)
             if first:
                 acc[pl.ds(at, chunk), cols(h)] = part
@@ -154,65 +183,55 @@
     def p_send(h, m):
         to = partner(r, m)
         return remote(
-            pout.at[to, :, cols(h)], pin.at[r, :, cols(h)], ps.at[h, m], pr.at[h, r], to, b
-        )
-
-    for h in range(pieces):
-        add_panel(h, b * slab, slab, xg[b, :, cols(h)], True)
-        arrive(xg.at[other, :, cols(h)], xs.at[h, 1, 0], xr.at[h, other], r, other)
-        add_panel(h, other * slab, slab, xg[other, :, cols(h)], False)
+            pout.at[to, h], pin.at[r, h], ps.at[h, m], pr.at[h, r], to, b
+        )
+
+    for h in range(pieces):
+        add_panel(dense, h, b * slab, slab, xg[b, h], True)
+        arrive(xg.at[other, h], xs.at[h, 1, 0], xr.at[h, other], r, other)
+        add_panel(dense, h, other * slab, slab, xg[other, h], False)
         for m in range(1, line):
             blk = blk_at(m)
-            arrive(xg.at[blk, :, cols(h)], xs.at[h, 0, m], xr.at[h, blk], r, blk)
+            arrive(xg.at[blk, h], xs.at[h, 0, m], xr.at[h, blk], r, blk)
             if relay and m == 2:
                 @pl.when(jnp.logical_not(outer))
                 def _():
                     x_relay(h).start()
             x_pass(h, m).start()
-            add_panel(h, blk * slab, slab, xg[blk, :, cols(h)], False)
+            add_panel(dense, h, blk * slab, slab, xg[blk, h], False)
+            if early and later:
+                later.pop(0)()
             if m > 1:
                 last = partner(z, m - 1) * 2 + 1 - c
-                arrive(xg.at[last, :, cols(h)], xs.at[h, 1, m - 1], xr.at[h, last], r, other)
-                add_panel(h, last * slab, slab, xg[last, :, cols(h)], False)
+                arrive(xg.at[last, h], xs.at[h, 1, m - 1], xr.at[h, last], r, other)
+                add_panel(dense, h, last * slab, slab, xg[last, h], False)
         last = partner(z, line - 1) * 2 + 1 - c
-        arrive(xg.at[last, :, cols(h)], xs.at[h, 1, line - 1], xr.at[h, last], r, other)
+        arrive(xg.at[last, h], xs.at[h, 1, line - 1], xr.at[h, last], r, other)
         for m in range(n_rep - 1, -1, -1):
             to = partner(r, m)
             at = pl.multiple_of(to * rows, rows)
             panel = dense[pl.ds(pl.multiple_of(last * slab + to * rows, rows), rows), :]
             part = acc[pl.ds(at, rows), cols(h)] + jnp.dot(
-                panel, xg[last, :, cols(h)], preferred_element_type=F32
+                panel, xg[last, h], preferred_element_type=F32
             )
-            pout[to, :, cols(h)] = part.astype(BF16)
+            pout[to, h] = part.astype(BF16)
             if m:
                 p_send(h, m).start()
 
-    def turn(t, carry):
-        tiles[t] = tiles[t].T
-        return carry
-
-    lax.fori_loop(1, tiles.shape[0], turn, 0)
-
-    def lay_out_turned(n, carry):
-        panel, k = n // group_blocks, n % group_blocks
-        for j in range(per):
-            slot = slot_at((panel * per + j) * group_blocks + k)
-            start = pl.multiple_of(panel * group + k * tile, tile)
-            dense[pl.ds(start, tile), j * tile:(j + 1) * tile] = tiles[slot]
-        return carry
-
-    lax.fori_loop(0, n_rep * group_blocks, lay_out_turned, 0, unroll=4)
+    while later:
+        later.pop(0)()
+    fetch[1].wait()
     fetch[2].wait()
-    fetch[3].wait()
-
-    total = pout[r].astype(F32)
-    for m in range(1, n_rep):
-        peer = partner(r, m)
-        for h in range(pieces):
-            arrive(pin.at[peer, :, cols(h)], ps.at[h, m], pr.at[h, peer], peer, b)
-        total = total + pin[peer].astype(F32)
-    hidden = total.astype(BF16)
-    preact = jnp.dot(hidden, w[...], preferred_element_type=F32)
+
+    hidden, preact = [], 0.0
+    for h in range(pieces):
+        total = pout[r, h].astype(F32)
+        for m in range(1, n_rep):
+            peer = partner(r, m)
+            arrive(pin.at[peer, h], ps.at[h, m], pr.at[h, peer], peer, b)
+            total = total + pin[peer, h].astype(F32)
+        hidden.append(total.astype(BF16))
+        preact += jnp.dot(hidden[h], w[cols(h), :], preferred_element_type=F32)
     gate = jax.nn.sigmoid(preact)
     slope = gate * (1.0 + preact * (1.0 - gate))
     grad_pre = (cot[...].astype(F32) * slope).astype(BF16)
@@ -220,11 +239,11 @@
     def g_send(h, m):
         to = partner(r, m)
         return remote(
-            gg.at[r, :, cols(h)], gg.at[r, :, cols(h)], gs.at[h, m], gr.at[h, r], to, b
-        )
-
-    for h in range(pieces):
-        gg[r, :, cols(h)] = lax.dot_general(
+            gg.at[r, h], gg.at[r, h], gs.at[h, m], gr.at[h, r], to, b
+        )
+
+    for h in range(pieces):
+        gg[r, h] = lax.dot_general(
             grad_pre, w[cols(h), :], (((1,), (1,)), ((), ())), preferred_element_type=F32
         ).astype(BF16)
         for m in range(n_rep - 1, 0, -1):
@@ -233,9 +252,10 @@
     layer_ref[...] = (preact * gate).astype(BF16)
     layer_out = pltpu.make_async_copy(layer_ref, layer_hbm, loc.at[5])
     layer_out.start()
-    wpart[...] = lax.dot_general(
-        hidden, grad_pre, (((0,), (0,)), ((), ())), preferred_element_type=F32
-    )
+    for h in range(pieces):
+        wpart[cols(h), :] = lax.dot_general(
+            hidden[h], grad_pre, (((0,), (0,)), ((), ())), preferred_element_type=F32
+        )
     half = feats // 2
     share = half // line
     kind = wl_out.dtype
@@ -244,7 +264,7 @@
     w_sib = remote(wsib_out, wsib_in, ws.at[0, 0], wr.at[0, 0], r, other)
     w_sib.start()
 
-    add_panel(0, r * group, group, gg[r, :, cols(0)], True)
+    add_panel(turned, 0, r * group, group, gg[r, 0], True)
 
     w_sib.wait_recv()
     both = wpart[pl.ds(pl.multiple_of(mine_at, half), half), :] + wsib_in[...].astype(F32)
@@ -299,60 +319,55 @@
     def b_sib(h, m):
         place = partner(z, m)
         return remote(
-            bsib_out.at[place, :, cols(h)], bsib_in.at[place, :, cols(h)],
+            bsib_out.at[place, h], bsib_in.at[place, h],
             bs.at[h, 0, m], br_sib.at[h, place], r, other,
         )
 
     def b_line(h, m):
         return remote(
-            bout.at[m, :, cols(h)], bin_.at[m, :, cols(h)],
+            bout.at[m, h], bin_.at[m, h],
             bs.at[h, 1, m], br_line.at[h, m], r, blk_at(m),
         )
 
     def b_relay(h):
         return remote(
-            bout.at[3, :, cols(h)], brelay.at[:, cols(h)],
+            bout.at[3, h], brelay.at[h],
             bs.at[h, 1, 3], br_relay.at[h], r, blk_at(2),
         )
 
-    for h in range(pieces):
+    tail = n_rep - 1
+
+    def finish(h, blk):
+        peer = partner(r, tail)
+        at = pl.multiple_of(blk * rows, rows)
+        panel = turned[pl.ds(pl.multiple_of(peer * group + blk * rows, rows), rows), :]
+        return acc[pl.ds(at, rows), cols(h)] + jnp.dot(
+            panel, gg[peer, h], preferred_element_type=F32
+        )
+
+    def back_terms(h):
         if h:
-            add_panel(h, r * group, group, gg[r, :, cols(h)], True)
+            add_panel(turned, h, r * group, group, gg[r, h], True)
         for m in range(1, n_rep):
             peer = partner(r, m)
-            arrive(gg.at[peer, :, cols(h)], gs.at[h, m], gr.at[h, peer], peer, b)
-            if m < n_rep - 1:
-                add_panel(h, peer * group, group, gg[peer, :, cols(h)], False)
-            if m == 1 and h == 0:
-                w_sum_line()
-        peer = partner(r, n_rep - 1)
-        rhs = gg[peer, :, cols(h)]
-
-        def finish(blk):
-            at = pl.multiple_of(blk * rows, rows)
-            panel = dense[pl.ds(pl.multiple_of(peer * group + blk * rows, rows), rows), :]
-            return acc[pl.ds(at, rows), cols(h)] + jnp.dot(
-                panel, rhs, preferred_element_type=F32
-            )
-
+            arrive(gg.at[peer, h], gs.at[h, m], gr.at[h, peer], peer, b)
+            if m < tail:
+                add_panel(turned, h, peer * group, group, gg[peer, h], False)
         for m in range(line - 1, -1, -1):
             place = partner(z, m)
-            bsib_out[place, :, cols(h)] = finish(place * 2 + 1 - c).astype(BF16)
+            bsib_out[place, h] = finish(h, place * 2 + 1 - c).astype(BF16)
             b_sib(h, m).start()
-        if h == pieces - 1:
-            w_sum_rep()
-        for m in range(line - 1, -1, -1):
-            place = partner(z, m)
-            mine = finish(place * 2 + c)
-            arrive(
-                bsib_in.at[place, :, cols(h)], bs.at[h, 0, m], br_sib.at[h, place], r, other
-            )
-            mine = mine + bsib_in[place, :, cols(h)].astype(F32)
-            if m == 0:
-                fin[0, :, cols(h)] = mine
-            elif relay and m == 3:
-                bout[m, :, cols(h)] = mine.astype(BF16)
-
+
+    def chip_sum(h, m):
+        place = partner(z, m)
+        mine = finish(h, place * 2 + c)
+        arrive(bsib_in.at[place, h], bs.at[h, 0, m], br_sib.at[h, place], r, other)
+        return mine + bsib_in[place, h].astype(F32)
+
+    def send_far(h):
+        for m in range(line - 1, 1, -1):
+            bout[m, h] = chip_sum(h, m).astype(BF16)
+            if relay and m == 3:
                 @pl.when(outer)
                 def _():
                     b_relay(h).start()
@@ -360,19 +375,31 @@
                 @pl.when(jnp.logical_not(outer))
                 def _():
                     b_line(h, m).start()
-            elif relay and m == 1:
-                fin[1, :, cols(h)] = mine
-
-                @pl.when(jnp.logical_not(outer))
-                def _():
-                    b_relay(h).wait_recv()
-                    fin[1, :, cols(h)] += brelay[:, cols(h)].astype(F32)
-
-                bout[m, :, cols(h)] = fin[1, :, cols(h)].astype(BF16)
+            else:
                 b_line(h, m).start()
-            else:
-                bout[m, :, cols(h)] = mine.astype(BF16)
-                b_line(h, m).start()
+        fin[1, :, cols(h)] = chip_sum(h, 1)
+        fin[0, :, cols(h)] = chip_sum(h, 0)
+
+    def send_near(h):
+        if relay:
+            @pl.when(jnp.logical_not(outer))
+            def _():
+                b_relay(h).wait_recv()
+                fin[1, :, cols(h)] += brelay[h].astype(F32)
+
+        bout[1, h] = fin[1, :, cols(h)].astype(BF16)
+        b_line(h, 1).start()
+
+    for h in range(pieces):
+        back_terms(h)
+        if h == 0:
+            w_sum_line()
+        else:
+            send_near(h - 1)
+        if h == pieces - 1:
+            w_sum_rep()
+        send_far(h)
+    send_near(pieces - 1)
 
     for m in range(1, line):
         place = partner(z, m)
@@ -394,10 +421,10 @@
                 @pl.when(jnp.logical_not(outer))
                 def _():
                     b_line(h, m).wait_recv()
-                    fin[0, :, cols(h)] += bin_[m, :, cols(h)].astype(F32)
+                    fin[0, :, cols(h)] += bin_[m, h].astype(F32)
             else:
                 b_line(h, m).wait_recv()
-                fin[0, :, cols(h)] += bin_[m, :, cols(h)].astype(F32)
+                fin[0, :, cols(h)] += bin_[m, h].astype(F32)
     gf_ref[...] = fin[0].astype(BF16)
     gf_out = pltpu.make_async_copy(gf_ref, gf_hbm, loc.at[7])
     gf_out.start()
@@ -432,14 +459,16 @@
         copy.wait()
 
 
-def hand_over(layer, gw, gf, layer_to, gw_to, gf_to, sems):
-    copies = [
-        pltpu.make_async_copy(src, dst, sems.at[i])
-        for i, (src, dst) in enumerate([(layer, layer_to), (gw, gw_to), (gf, gf_to)])
-    ]
-    for copy in copies:
+def hand_over(layer, gw, gf, layer_to, gw_to, gf_to, layer_at, gw_at, gf_at, sems):
+    trips = [(layer, layer_at, layer_to), (gw, gw_at, gw_to), (gf, gf_at, gf_to)]
+    inward = [pltpu.make_async_copy(a, b, sems.at[0, i]) for i, (a, b, _) in enumerate(trips)]
+    outward = [pltpu.make_async_copy(b, c, sems.at[1, i]) for i, (_, b, c) in enumerate(trips)]
+    for copy in inward:
         copy.start()
-    for copy in copies:
+    for first, second in zip(inward, outward):
+        first.wait()
+        second.start()
+    for copy in outward:
         copy.wait()
 
 
@@ -455,6 +484,9 @@
     table = (-(-pairs // 1024) * 8, 128)
     block = (rows, feats)
     h = PIECES
+    piece = (h, rows, feats // h)
+    slab_size = n_blk * n_rep * rows
+    copies = 2 if slab_size * rows * 4 <= 24 * 1024 * 1024 else 1
     dma = pltpu.SemaphoreType.DMA
     results = (
         jax.ShapeDtypeStruct(block, BF16),
@@ -475,19 +507,19 @@
             pltpu.VMEM((feats, feats), F32),
             pltpu.VMEM(block, BF16),
             pltpu.VMEM((slots + 1, tile, tile), BF16),
-            pltpu.VMEM((n_blk * n_rep * rows, rows), BF16),
-            pltpu.VMEM((n_blk,) + block, BF16),
+            pltpu.VMEM((copies, slab_size, rows), BF16),
+            pltpu.VMEM((n_blk,) + piece, BF16),
             pltpu.VMEM((feats, feats), BF16),
             pltpu.VMEM(block, BF16),
             pltpu.VMEM((max(n_blk, n_rep) * rows, feats), F32),
-            pltpu.VMEM((n_rep,) + block, BF16),
-            pltpu.VMEM((n_rep,) + block, BF16),
-            pltpu.VMEM((n_rep,) + block, BF16),
-            pltpu.VMEM((line,) + block, BF16),
-            pltpu.VMEM((line,) + block, BF16),
-            pltpu.VMEM((line,) + block, BF16),
-            pltpu.VMEM((line,) + block, BF16),
-            pltpu.VMEM(block, BF16),
+            pltpu.VMEM((n_rep,) + piece, BF16),
+            pltpu.VMEM((n_rep,) + piece, BF16),
+            pltpu.VMEM((n_rep,) + piece, BF16),
+            pltpu.VMEM((line,) + piece, BF16),
+            pltpu.VMEM((line,) + piece, BF16),
+            pltpu.VMEM((line,) + piece, BF16),
+            pltpu.VMEM((line,) + piece, BF16),
+            pltpu.VMEM(piece, BF16),
             pltpu.VMEM((feats // 2, feats), kind),
             pltpu.VMEM((feats // 2, feats), kind),
             pltpu.VMEM((line, share, feats), kind),
@@ -496,7 +528,7 @@
             pltpu.VMEM((2, line, share, feats), kind),
             pltpu.VMEM((feats, feats), F32),
             pltpu.VMEM((2,) + block, F32),
-            dma((8,)),
+            dma((8 + h,)),
             dma((h, 2, line)),
             dma((h, n_blk)),
             dma((h, n_rep)),
@@ -522,7 +554,7 @@
         out_shape=results,
         in_specs=[anywhere] * 3,
         out_specs=(anywhere,) * 3,
-        scratch_shapes=[dma((3,))],
+        scratch_shapes=[pltpu.VMEM(made[i].shape, made[i].dtype) for i in range(3)] + [dma((2, 3))],
         compiler_params=pltpu.CompilerParams(vmem_limit_bytes=62 * 1024 * 1024),
     )(*made)
     return layer.reshape((1, 1) + block), gw, gf

time: 68.8 us -> 53.7 us (0.78)
  Pallas kernels: 67.3 us -> 52.2 us
    pallas_call x1, Pallas kernels: 17 us -> 1.81 us  [on_device(): pl.pallas_call(hand_over, out_shape=results, in_specs=[anywhere] * 3, out...]
where the time goes in v4:
time: 53.7 us; the launch traced here: 53.5 us
  Pallas kernels  52.2 us (97%)
  between operations  1.29 us (2%)
    pallas_call x1, Pallas kernels, on_device(): pl.pallas_call(functools.partial(kernel, n_rep, n_blk, h), out_shape=resu...  50.4 us
    pallas_call x1, Pallas kernels, on_device(): pl.pallas_call(hand_over, out_shape=results, in_specs=[anywhere] * 3, out...  1.81 us

profile of v4, /device:TPU:0, one launch (start us, length us, event | category | flops | bytes accessed | tf_op | source)
XLA Modules:
  0.0 53.5 jit_solution(12184649977532958518)
XLA Ops:
  1.3 50.4 %shard_map.94 = (bf16[256,256]{1,0:T(8,128)(2,1)}, f32[256,256]{1,0:T(8,128)}, bf16[256,256]{1,0:T(8,128)(2,1)}) custom-call(s32[16]{0:T(128)} %bitcast.7, s32[16]{0:T(128)} %bitcast.8, s32[1,1]{1,0:T(1,128)S(6)} %copy.10.count_ref, bf16[16,128,128]{2,1,0:T(8,128)(2,1)} %bitcast.5, bf16[256,256]{1,0:T(8,128)(2,1)} %x_hbm.1, bf16[256,256]{1,0:T(8,128)(2,1)} %w_hbm.1, ...), custom_call_target="tpu_custom_call" | custom-call | tf_op jit(solution)/shard_map/pallas_call | solution.py:498
  51.7 1.8 %shard_map.95 = (bf16[256,256]{1,0:T(8,128)(2,1)}, f32[256,256]{1,0:T(8,128)}, bf16[256,256]{1,0:T(8,128)(2,1)}) custom-call(bf16[256,256]{1,0:T(8,128)(2,1)} %get-tuple-element.9.layer, f32[256,256]{1,0:T(8,128)} %get-tuple-element.10.gw, bf16[256,256]{1,0:T(8,128)(2,1)} %get-tuple-element.11.gf), custom_call_target="tpu_custom_call" | custom-call | tf_op jit(solution)/shard_map/pallas_call | solution.py:552

commit v5 on v4

--- a/solution.py
+++ b/solution.py
@@ -10,14 +10,17 @@
 MESH = pl.DeviceIdType.MESH
 BF16, F32 = jnp.bfloat16, jnp.float32
 PIECES = 2
-
-
-def partner(index, step):
-    out, bit = index, 1
-    while bit <= step:
-        if step & bit:
-            out = out + bit * (1 - 2 * ((index // bit) % 2))
-        bit *= 2
+CHUNK = 256
+
+
+def partner(index, step, bits=8):
+    out = index
+    for bit in [2**i for i in range(bits)]:
+        flip = 1 - 2 * ((index // bit) % 2)
+        if isinstance(step, int):
+            out = out + bit * flip if step & bit else out
+        else:
+            out = out + bit * flip * ((step // bit) % 2)
     return out
 
 
@@ -142,7 +145,7 @@
             dense[pl.ds(start, tile), j * tile:(j + 1) * tile] = tiles[slot]
         return carry
 
-    lax.fori_loop(0, n_blk * slab_blocks, lay_out, 0, unroll=4)
+    lax.fori_loop(0, n_blk * slab_blocks, lay_out, 0, unroll=2)
 
     def turn(t, carry):
         tiles[t] = tiles[t].T
@@ -165,31 +168,33 @@
             for i in range(count)
         ]
 
-    later = steps(turn, 1, tiles.shape[0], 2, 2)
-    later += steps(lay_out_turned, 0, n_rep * group_blocks, 4, 4)
+    later = steps(turn, 1, tiles.shape[0], 2, 1)
+    later += steps(lay_out_turned, 0, n_rep * group_blocks, 4, 2)
     early = slabs.shape[0] > 1
 
-    chunk = 4 * rows if slab % (4 * rows) == 0 else rows
-
-    def add_panel(slabs, h, base, height, rhs, first):
-        for at in range(0, height, chunk):
-            lhs = slabs[pl.ds(pl.multiple_of(base + at, tile), chunk), :]
-            part = jnp.dot(lhs, rhs, preferred_element_type=F32)
+    def add_panel(slab_ref, h, base, height, rhs_ref, first):
+        def add(i, carry):
+            at = pl.multiple_of(i * CHUNK, CHUNK)
+            lhs = slab_ref[pl.ds(pl.multiple_of(base + i * CHUNK, tile), CHUNK), :]
+            part = jnp.dot(lhs, rhs_ref[...], preferred_element_type=F32)
             if first:
-                acc[pl.ds(at, chunk), cols(h)] = part
+                acc[pl.ds(at, CHUNK), cols(h)] = part
             else:
-                acc[pl.ds(at, chunk), cols(h)] += part
+                acc[pl.ds(at, CHUNK), cols(h)] += part
+            return carry
+
+        lax.fori_loop(0, height // CHUNK, add, 0)
 
     def p_send(h, m):
-        to = partner(r, m)
+        to = partner(r, m, 3)
         return remote(
             pout.at[to, h], pin.at[r, h], ps.at[h, m], pr.at[h, r], to, b
         )
 
     for h in range(pieces):
-        add_panel(dense, h, b * slab, slab, xg[b, h], True)
+        add_panel(dense, h, b * slab, slab, xg.at[b, h], True)
         arrive(xg.at[other, h], xs.at[h, 1, 0], xr.at[h, other], r, other)
-        add_panel(dense, h, other * slab, slab, xg[other, h], False)
+        add_panel(dense, h, other * slab, slab, xg.at[other, h], False)
         for m in range(1, line):
             blk = blk_at(m)
             arrive(xg.at[blk, h], xs.at[h, 0, m], xr.at[h, blk], r, blk)
@@ -198,25 +203,32 @@
                 def _():
                     x_relay(h).start()
             x_pass(h, m).start()
-            add_panel(dense, h, blk * slab, slab, xg[blk, h], False)
+            add_panel(dense, h, blk * slab, slab, xg.at[blk, h], False)
             if early and later:
                 later.pop(0)()
             if m > 1:
                 last = partner(z, m - 1) * 2 + 1 - c
                 arrive(xg.at[last, h], xs.at[h, 1, m - 1], xr.at[h, last], r, other)
-                add_panel(dense, h, last * slab, slab, xg[last, h], False)
+                add_panel(dense, h, last * slab, slab, xg.at[last, h], False)
         last = partner(z, line - 1) * 2 + 1 - c
         arrive(xg.at[last, h], xs.at[h, 1, line - 1], xr.at[h, last], r, other)
-        for m in range(n_rep - 1, -1, -1):
-            to = partner(r, m)
+        def last_panel(i, carry):
+            m = n_rep - 1 - i
+            to = partner(r, m, 3)
             at = pl.multiple_of(to * rows, rows)
             panel = dense[pl.ds(pl.multiple_of(last * slab + to * rows, rows), rows), :]
             part = acc[pl.ds(at, rows), cols(h)] + jnp.dot(
                 panel, xg[last, h], preferred_element_type=F32
             )
             pout[to, h] = part.astype(BF16)
-            if m:
+
+            @pl.when(m > 0)
+            def _():
                 p_send(h, m).start()
+
+            return carry
+
+        lax.fori_loop(0, n_rep, last_panel, 0)
 
     while later:
         later.pop(0)()
@@ -264,7 +276,7 @@
     w_sib = remote(wsib_out, wsib_in, ws.at[0, 0], wr.at[0, 0], r, other)
     w_sib.start()
 
-    add_panel(turned, 0, r * group, group, gg[r, 0], True)
+    add_panel(turned, 0, r * group, group, gg.at[r, 0], True)
 
     w_sib.wait_recv()
     both = wpart[pl.ds(pl.multiple_of(mine_at, half), half), :] + wsib_in[...].astype(F32)
@@ -317,7 +329,7 @@
         w_pass(0).start()
 
     def b_sib(h, m):
-        place = partner(z, m)
+        place = partner(z, m, 4)
         return remote(
             bsib_out.at[place, h], bsib_in.at[place, h],
             bs.at[h, 0, m], br_sib.at[h, place], r, other,
@@ -347,20 +359,31 @@
 
     def back_terms(h):
         if h:
-            add_panel(turned, h, r * group, group, gg[r, h], True)
+            add_panel(turned, h, r * group, group, gg.at[r, h], True)
         for m in range(1, n_rep):
             peer = partner(r, m)
             arrive(gg.at[peer, h], gs.at[h, m], gr.at[h, peer], peer, b)
             if m < tail:
-                add_panel(turned, h, peer * group, group, gg[peer, h], False)
-        for m in range(line - 1, -1, -1):
-            place = partner(z, m)
+                add_panel(turned, h, peer * group, group, gg.at[peer, h], False)
+
+        def to_sibling(i, carry):
+            m = line - 1 - i
+            place = partner(z, m, 4)
             bsib_out[place, h] = finish(h, place * 2 + 1 - c).astype(BF16)
             b_sib(h, m).start()
+            return carry
+
+        def keep(i, carry):
+            blk = i * 2 + c
+            acc[pl.ds(pl.multiple_of(blk * rows, rows), rows), cols(h)] = finish(h, blk)
+            return carry
+
+        lax.fori_loop(0, line, to_sibling, 0)
+        lax.fori_loop(0, line, keep, 0)
 
     def chip_sum(h, m):
         place = partner(z, m)
-        mine = finish(h, place * 2 + c)
+        mine = acc[pl.ds(pl.multiple_of((place * 2 + c) * rows, rows), rows), cols(h)]
         arrive(bsib_in.at[place, h], bs.at[h, 0, m], br_sib.at[h, place], r, other)
         return mine + bsib_in[place, h].astype(F32)
 

time: 53.7 us -> 60.6 us (1.13)
  Pallas kernels: 52.2 us -> 59.2 us
    pallas_call x1, Pallas kernels: 50.4 us -> 57.4 us  [on_device(): pl.pallas_call(functools.partial(kernel, n_rep, n_blk, h), out_shape=resu...]
where the time goes in v5:
time: 60.6 us; the launch traced here: 60.5 us
  Pallas kernels  59.2 us (98%)
  between operations  1.29 us (2%)
    pallas_call x1, Pallas kernels, on_device(): pl.pallas_call(functools.partial(kernel, n_rep, n_blk, h), out_shape=resu...  57.4 us
    pallas_call x1, Pallas kernels, on_device(): pl.pallas_call(hand_over, out_shape=results, in_specs=[anywhere] * 3, out...  1.81 us

profile of v5, /device:TPU:0, one launch (start us, length us, event | category | flops | bytes accessed | tf_op | source)
XLA Modules:
  0.0 60.5 jit_solution(17632236991540673260)
XLA Ops:
  1.3 57.4 %shard_map.94 = (bf16[256,256]{1,0:T(8,128)(2,1)}, f32[256,256]{1,0:T(8,128)}, bf16[256,256]{1,0:T(8,128)(2,1)}) custom-call(s32[16]{0:T(128)} %bitcast.7, s32[16]{0:T(128)} %bitcast.8, s32[1,1]{1,0:T(1,128)S(6)} %copy.10.count_ref, bf16[16,128,128]{2,1,0:T(8,128)(2,1)} %bitcast.5, bf16[256,256]{1,0:T(8,128)(2,1)} %x_hbm.1, bf16[256,256]{1,0:T(8,128)(2,1)} %w_hbm.1, ...), custom_call_target="tpu_custom_call" | custom-call | tf_op jit(solution)/shard_map/pallas_call | solution.py:521
  58.6 1.8 %shard_map.95 = (bf16[256,256]{1,0:T(8,128)(2,1)}, f32[256,256]{1,0:T(8,128)}, bf16[256,256]{1,0:T(8,128)(2,1)}) custom-call(bf16[256,256]{1,0:T(8,128)(2,1)} %get-tuple-element.9.layer, f32[256,256]{1,0:T(8,128)} %get-tuple-element.10.gw, bf16[256,256]{1,0:T(8,128)(2,1)} %get-tuple-element.11.gf), custom_call_target="tpu_custom_call" | custom-call | tf_op jit(solution)/shard_map/pallas_call | solution.py:575

commit v6 on v4

--- a/solution.py
+++ b/solution.py
@@ -142,7 +142,7 @@
             dense[pl.ds(start, tile), j * tile:(j + 1) * tile] = tiles[slot]
         return carry
 
-    lax.fori_loop(0, n_blk * slab_blocks, lay_out, 0, unroll=4)
+    lax.fori_loop(0, n_blk * slab_blocks, lay_out, 0, unroll=8)
 
     def turn(t, carry):
         tiles[t] = tiles[t].T
@@ -165,8 +165,8 @@
             for i in range(count)
         ]
 
-    later = steps(turn, 1, tiles.shape[0], 2, 2)
-    later += steps(lay_out_turned, 0, n_rep * group_blocks, 4, 4)
+    later = steps(turn, 1, tiles.shape[0], 2, 4)
+    later += steps(lay_out_turned, 0, n_rep * group_blocks, 4, 8)
     early = slabs.shape[0] > 1
 
     chunk = 4 * rows if slab % (4 * rows) == 0 else rows
@@ -186,10 +186,23 @@
             pout.at[to, h], pin.at[r, h], ps.at[h, m], pr.at[h, r], to, b
         )
 
-    for h in range(pieces):
-        add_panel(dense, h, b * slab, slab, xg[b, h], True)
+    span = min(n_blk, 8)
+
+    def partial_rows(h, to):
+        def add(first, total):
+            for i in range(span):
+                blk = first * span + i
+                at = pl.multiple_of(blk * slab + to * rows, rows)
+                total += jnp.dot(
+                    dense[pl.ds(at, rows), :], xg[blk, h], preferred_element_type=F32
+                )
+            return total
+
+        zero = jnp.zeros((rows, fh), F32)
+        return add(0, zero) if span == n_blk else lax.fori_loop(0, n_blk // span, add, zero)
+
+    for h in range(pieces):
         arrive(xg.at[other, h], xs.at[h, 1, 0], xr.at[h, other], r, other)
-        add_panel(dense, h, other * slab, slab, xg[other, h], False)
         for m in range(1, line):
             blk = blk_at(m)
             arrive(xg.at[blk, h], xs.at[h, 0, m], xr.at[h, blk], r, blk)
@@ -198,23 +211,15 @@
                 def _():
                     x_relay(h).start()
             x_pass(h, m).start()
-            add_panel(dense, h, blk * slab, slab, xg[blk, h], False)
-            if early and later:
+            if early and later and h == 0:
                 later.pop(0)()
-            if m > 1:
-                last = partner(z, m - 1) * 2 + 1 - c
-                arrive(xg.at[last, h], xs.at[h, 1, m - 1], xr.at[h, last], r, other)
-                add_panel(dense, h, last * slab, slab, xg[last, h], False)
-        last = partner(z, line - 1) * 2 + 1 - c
-        arrive(xg.at[last, h], xs.at[h, 1, line - 1], xr.at[h, last], r, other)
+                later.pop(0)()
+        for m in range(1, line):
+            last = partner(z, m) * 2 + 1 - c
+            arrive(xg.at[last, h], xs.at[h, 1, m], xr.at[h, last], r, other)
         for m in range(n_rep - 1, -1, -1):
             to = partner(r, m)
-            at = pl.multiple_of(to * rows, rows)
-            panel = dense[pl.ds(pl.multiple_of(last * slab + to * rows, rows), rows), :]
-            part = acc[pl.ds(at, rows), cols(h)] + jnp.dot(
-                panel, xg[last, h], preferred_element_type=F32
-            )
-            pout[to, h] = part.astype(BF16)
+            pout[to, h] = partial_rows(h, to).astype(BF16)
             if m:
                 p_send(h, m).start()
 
@@ -340,18 +345,22 @@
     def finish(h, blk):
         peer = partner(r, tail)
         at = pl.multiple_of(blk * rows, rows)
-        panel = turned[pl.ds(pl.multiple_of(peer * group + blk * rows, rows), rows), :]
-        return acc[pl.ds(at, rows), cols(h)] + jnp.dot(
-            panel, gg[peer, h], preferred_element_type=F32
-        )
+        if h == 0:
+            panel = turned[pl.ds(pl.multiple_of(peer * group + blk * rows, rows), rows), :]
+            return acc[pl.ds(at, rows), cols(h)] + jnp.dot(
+                panel, gg[peer, h], preferred_element_type=F32
+            )
+        total = jnp.zeros((rows, fh), F32)
+        for rep in range(n_rep):
+            panel = turned[pl.ds(pl.multiple_of(rep * group + blk * rows, rows), rows), :]
+            total += jnp.dot(panel, gg[rep, h], preferred_element_type=F32)
+        return total
 
     def back_terms(h):
-        if h:
-            add_panel(turned, h, r * group, group, gg[r, h], True)
         for m in range(1, n_rep):
             peer = partner(r, m)
             arrive(gg.at[peer, h], gs.at[h, m], gr.at[h, peer], peer, b)
-            if m < tail:
+            if m < tail and h == 0:
                 add_panel(turned, h, peer * group, group, gg[peer, h], False)
         for m in range(line - 1, -1, -1):
             place = partner(z, m)

time: 53.7 us -> 52.8 us (0.983)
  Pallas kernels: 52.2 us -> 51.3 us
    pallas_call x1, Pallas kernels: 50.4 us -> 49.5 us  [on_device(): pl.pallas_call(functools.partial(kernel, n_rep, n_blk, h), out_shape=resu...]
where the time goes in v6:
time: 52.8 us; the launch traced here: 52.6 us
  Pallas kernels  51.3 us (97%)
  between operations  1.29 us (2%)
    pallas_call x1, Pallas kernels, on_device(): pl.pallas_call(functools.partial(kernel, n_rep, n_blk, h), out_shape=resu...  49.5 us
    pallas_call x1, Pallas kernels, on_device(): pl.pallas_call(hand_over, out_shape=results, in_specs=[anywhere] * 3, out...  1.81 us

profile of v6, /device:TPU:0, one launch (start us, length us, event | category | flops | bytes accessed | tf_op | source)
XLA Modules:
  0.0 52.6 jit_solution(4297096435630109739)
XLA Ops:
  1.3 49.5 %shard_map.94 = (bf16[256,256]{1,0:T(8,128)(2,1)}, f32[256,256]{1,0:T(8,128)}, bf16[256,256]{1,0:T(8,128)(2,1)}) custom-call(s32[16]{0:T(128)} %bitcast.7, s32[16]{0:T(128)} %bitcast.8, s32[1,1]{1,0:T(1,128)S(6)} %copy.10.count_ref, bf16[16,128,128]{2,1,0:T(8,128)(2,1)} %bitcast.5, bf16[256,256]{1,0:T(8,128)(2,1)} %x_hbm.1, bf16[256,256]{1,0:T(8,128)(2,1)} %w_hbm.1, ...), custom_call_target="tpu_custom_call" | custom-call | tf_op jit(solution)/shard_map/pallas_call | solution.py:507
  50.8 1.8 %shard_map.95 = (bf16[256,256]{1,0:T(8,128)(2,1)}, f32[256,256]{1,0:T(8,128)}, bf16[256,256]{1,0:T(8,128)(2,1)}) custom-call(bf16[256,256]{1,0:T(8,128)(2,1)} %get-tuple-element.9.layer, f32[256,256]{1,0:T(8,128)} %get-tuple-element.10.gw, bf16[256,256]{1,0:T(8,128)(2,1)} %get-tuple-element.11.gf), custom_call_target="tpu_custom_call" | custom-call | tf_op jit(solution)/shard_map/pallas_call | solution.py:561

commit v7 on v6

--- a/solution.py
+++ b/solution.py
@@ -165,9 +165,8 @@
             for i in range(count)
         ]
 
-    later = steps(turn, 1, tiles.shape[0], 2, 4)
-    later += steps(lay_out_turned, 0, n_rep * group_blocks, 4, 8)
-    early = slabs.shape[0] > 1
+    lax.fori_loop(1, tiles.shape[0], turn, 0, unroll=4)
+    later = steps(lay_out_turned, 0, n_rep * group_blocks, 4, 8)
 
     chunk = 4 * rows if slab % (4 * rows) == 0 else rows
 
@@ -211,9 +210,6 @@
                 def _():
                     x_relay(h).start()
             x_pass(h, m).start()
-            if early and later and h == 0:
-                later.pop(0)()
-                later.pop(0)()
         for m in range(1, line):
             last = partner(z, m) * 2 + 1 - c
             arrive(xg.at[last, h], xs.at[h, 1, m], xr.at[h, last], r, other)

time: 52.8 us -> 51.1 us (0.968)
  Pallas kernels: 51.3 us -> 49.7 us
    pallas_call x1, Pallas kernels: 49.5 us -> 47.9 us  [on_device(): pl.pallas_call(functools.partial(kernel, n_rep, n_blk, h), out_shape=resu...]
where the time goes in v7:
time: 51.1 us; the launch traced here: 51 us
  Pallas kernels  49.7 us (97%)
  between operations  1.29 us (3%)
    pallas_call x1, Pallas kernels, on_device(): pl.pallas_call(functools.partial(kernel, n_rep, n_blk, h), out_shape=resu...  47.9 us
    pallas_call x1, Pallas kernels, on_device(): pl.pallas_call(hand_over, out_shape=results, in_specs=[anywhere] * 3, out...  1.81 us

profile of v7, /device:TPU:0, one launch (start us, length us, event | category | flops | bytes accessed | tf_op | source)
XLA Modules:
  0.0 51.0 jit_solution(14251508300208778726)
XLA Ops:
  1.3 47.9 %shard_map.94 = (bf16[256,256]{1,0:T(8,128)(2,1)}, f32[256,256]{1,0:T(8,128)}, bf16[256,256]{1,0:T(8,128)(2,1)}) custom-call(s32[16]{0:T(128)} %bitcast.7, s32[16]{0:T(128)} %bitcast.8, s32[1,1]{1,0:T(1,128)S(6)} %copy.10.count_ref, bf16[16,128,128]{2,1,0:T(8,128)(2,1)} %bitcast.5, bf16[256,256]{1,0:T(8,128)(2,1)} %x_hbm.1, bf16[256,256]{1,0:T(8,128)(2,1)} %w_hbm.1, ...), custom_call_target="tpu_custom_call" | custom-call | tf_op jit(solution)/shard_map/pallas_call | solution.py:503
  49.1 1.8 %shard_map.95 = (bf16[256,256]{1,0:T(8,128)(2,1)}, f32[256,256]{1,0:T(8,128)}, bf16[256,256]{1,0:T(8,128)(2,1)}) custom-call(bf16[256,256]{1,0:T(8,128)(2,1)} %get-tuple-element.9.layer, f32[256,256]{1,0:T(8,128)} %get-tuple-element.10.gw, bf16[256,256]{1,0:T(8,128)(2,1)} %get-tuple-element.11.gf), custom_call_target="tpu_custom_call" | custom-call | tf_op jit(solution)/shard_map/pallas_call | solution.py:557
